TPU v7x, 32 devices: a whole 2x2x4 slice. The times are simulated.
32 devices in a mesh: groups: 2 (over y), seq: 16 (over z, x, core).
Axes of the slice: x: 2, y: 2, z: 4, core: 2. Of those that a mesh axis runs over, the one named last changes fastest.
Arguments:
- query_rows: bfloat16 [6144, 4096], P(('groups', 'seq')), parts along dimension 0, may hold values from -6 to 6
- key_rows: bfloat16 [6144, 512], P(('groups', 'seq')), parts along dimension 0, may hold values from -6 to 6
- value_rows: bfloat16 [6144, 512], P(('groups', 'seq')), parts along dimension 0, may hold values from -6 to 6
- keep_rank: int32 [32, 192], P(('groups', 'seq')), parts along dimension 0, may hold values from 0 to 191, each once within a row
- out_grad: bfloat16 [512, 4096], P(('groups', 'seq')), parts along dimension 0, may hold values from -6 to 6
Outputs:
- attended: bfloat16 [512, 4096], P(('groups', 'seq')), parts along dimension 0
- query_grad: bfloat16 [6144, 4096], P(('groups', 'seq')), parts along dimension 0
- key_grad: bfloat16 [6144, 512], P(('groups', 'seq')), parts along dimension 0
- value_grad: bfloat16 [6144, 512], P(('groups', 'seq')), parts along dimension 0
There are 2 independent parts, one for each index of `groups`. A program takes and returns all parts, laid end to end along the dimension named above; each array names one. Nothing has to cross between parts.
Inputs may be any that keep to these rules, and one draw needn't show every extreme that they name: Each row of keep_rank holds every number 0 to 191 once.
All inputs are finite; a program needn't handle non-finite values.
Results may differ from a plain program's by a relative error of at most 0.025.
Values may be sent and summed in bfloat16 or wider, within the bound.
A program may use at most 64 MiB of HBM per device.

v0:
```python
import jax
import jax.numpy as jnp
import numpy as np
from jax import lax
from jax.sharding import PartitionSpec as P

HEADS = 32
KVH = 4
HD = 128


def select_table(rank_row, kept_count):
    chosen = rank_row < kept_count
    slots = jnp.cumsum(chosen.astype(jnp.int32)) - 1
    target = jnp.where(chosen, slots, -1)
    wanted = jnp.arange(kept_count, dtype=jnp.int32)
    return (wanted[:, None] == target[None, :]).astype(jnp.bfloat16)


def to_units(row_block, row_parts):
    kept_count = row_block.shape[0]
    shaped = row_block.reshape(kept_count // row_parts, row_parts, HEADS, HD)
    return jnp.transpose(shaped, (2, 1, 0, 3)).reshape(
        HEADS * row_parts, kept_count // row_parts, HD
    )


def from_units(unit_block, row_parts):
    per_part = unit_block.shape[1]
    shaped = unit_block.reshape(HEADS, row_parts, per_part, HD)
    return jnp.transpose(shaped, (2, 1, 0, 3)).reshape(per_part * row_parts, HEADS * HD)


def body(query_rows, key_rows, value_rows, keep_rank, out_grad):
    shards = lax.axis_size("seq")
    my_index = lax.axis_index("seq")
    kept_count = out_grad.shape[0]
    head_width = HD
    kv_heads = KVH
    group_size = HEADS // kv_heads
    row_parts = max(1, shards // HEADS)
    unit_count = HEADS * row_parts // shards
    per_part = kept_count // row_parts
    key_total = shards * kept_count
    owner_rows = shards * per_part
    score_scale = HD ** (-0.5)
    selector = select_table(keep_rank[0], kept_count)
    q_kept = jnp.dot(selector, query_rows, preferred_element_type=jnp.float32).astype(jnp.bfloat16)
    both_rows = jnp.concatenate([key_rows, value_rows], axis=1)
    kv_kept = jnp.dot(selector, both_rows, preferred_element_type=jnp.float32).astype(jnp.bfloat16)
    q_units, g_units = (
        lax.all_to_all(to_units(q_kept, row_parts), "seq", split_axis=0, concat_axis=1, tiled=True),
        lax.all_to_all(
            to_units(out_grad, row_parts), "seq", split_axis=0, concat_axis=1, tiled=True
        ),
    )
    kv_head = my_index * unit_count // (row_parts * group_size)
    owners_head = np.arange(shards) * unit_count // (row_parts * group_size)
    gathered = lax.all_gather(kv_kept, "seq", axis=0, tiled=True)
    keys_here = lax.dynamic_slice_in_dim(gathered, kv_head * head_width, head_width, 1)
    values_here = lax.dynamic_slice_in_dim(
        gathered, (kv_heads + kv_head) * head_width, head_width, 1
    )
    step_src = 1
    while (
        step_src * 2 <= shards and shards % (step_src * 2) == 0 and (step_src * 2 * per_part <= 512)
    ):
        step_src = step_src * 2
    block_rows = step_src * per_part
    block_count = shards // step_src
    key_pos = jnp.arange(key_total, dtype=jnp.int32)
    offsets = jnp.arange(block_rows, dtype=jnp.int32)
    grad_keys = jnp.zeros((key_total, head_width), jnp.float32)
    grad_values = jnp.zeros((key_total, head_width), jnp.float32)
    out_list = []
    grad_list = []
    for unit in range(unit_count):
        part_here = (my_index * unit_count + unit) % row_parts
        unit_queries = q_units[unit]
        unit_grads = g_units[unit]

        def visit(block, state):
            out_all, grad_all, key_acc, value_acc = state
            source = block * step_src + offsets // per_part
            query_pos = source * kept_count + offsets % per_part * row_parts + part_here
            scores = (
                jnp.dot(unit_queries, keys_here.T, preferred_element_type=jnp.float32) * score_scale
            )
            scores = jnp.where(query_pos[:, None] >= key_pos[None, :], scores, -jnp.inf)
            row_top = jnp.max(scores, axis=1, keepdims=True)
            exponent = jnp.exp(scores - row_top)
            probs = exponent / jnp.sum(exponent, axis=1, keepdims=True)
            probs_low = probs.astype(jnp.bfloat16)
            out_block = jnp.dot(probs_low, values_here, preferred_element_type=jnp.float32).astype(
                jnp.bfloat16
            )
            grad_dot = jnp.sum(
                unit_grads.astype(jnp.float32) * out_block.astype(jnp.float32),
                axis=1,
                keepdims=True,
            )
            grad_prob = jnp.dot(unit_grads, values_here.T, preferred_element_type=jnp.float32)
            grad_score = (probs * (grad_prob - grad_dot)).astype(jnp.bfloat16)
            grad_query = (
                jnp.dot(grad_score, keys_here, preferred_element_type=jnp.float32) * score_scale
            ).astype(jnp.bfloat16)
            key_acc = (
                key_acc
                + jnp.dot(grad_score.T, unit_queries, preferred_element_type=jnp.float32)
                * score_scale
            )
            value_acc = value_acc + jnp.dot(
                probs_low.T, unit_grads, preferred_element_type=jnp.float32
            )
            out_all = out_block
            grad_all = grad_query
            return (out_all, grad_all, key_acc, value_acc)

        initial = (
            jnp.zeros((owner_rows, head_width), jnp.bfloat16),
            jnp.zeros((owner_rows, head_width), jnp.bfloat16),
            grad_keys,
            grad_values,
        )
        out_unit, grad_unit, grad_keys, grad_values = lax.fori_loop(0, block_count, visit, initial)
        out_list.append(out_unit)
        grad_list.append(grad_unit)
    out_back, grad_back = (
        lax.all_to_all(jnp.stack(out_list), "seq", split_axis=1, concat_axis=0, tiled=True),
        lax.all_to_all(jnp.stack(grad_list), "seq", split_axis=1, concat_axis=0, tiled=True),
    )
    attended = from_units(out_back, row_parts)
    query_kept = from_units(grad_back, row_parts)
    partial_value = jnp.concatenate([grad_keys, grad_values], axis=1).reshape(
        shards, kept_count, 2 * head_width
    )
    returned = lax.all_to_all(partial_value, "seq", split_axis=0, concat_axis=0, tiled=True)
    mixing = jnp.asarray(owners_head[:, None] == np.arange(kv_heads)[None, :], jnp.float32)
    summed = jnp.einsum("dkc,dg->kgc", returned, mixing, precision=lax.Precision.HIGHEST)
    key_kept = (
        summed[:, :, :head_width].reshape(kept_count, kv_heads * head_width).astype(jnp.bfloat16)
    )
    value_kept = (
        summed[:, :, head_width:].reshape(kept_count, kv_heads * head_width).astype(jnp.bfloat16)
    )
    spread = selector.T
    query_grad = jnp.dot(spread, query_kept, preferred_element_type=jnp.float32).astype(
        jnp.bfloat16
    )
    key_grad = jnp.dot(spread, key_kept, preferred_element_type=jnp.float32).astype(jnp.bfloat16)
    value_grad = jnp.dot(spread, value_kept, preferred_element_type=jnp.float32).astype(
        jnp.bfloat16
    )
    return (attended, query_grad, key_grad, value_grad)


def solution(mesh):
    return jax.shard_map(
        body,
        mesh=mesh,
        in_specs=(
            P(("groups", "seq"), None),
            P(("groups", "seq"), None),
            P(("groups", "seq"), None),
            P(("groups", "seq"), None),
            P(("groups", "seq"), None),
        ),
        out_specs=(
            P(("groups", "seq"), None),
            P(("groups", "seq"), None),
            P(("groups", "seq"), None),
            P(("groups", "seq"), None),
        ),
        check_vma=False,
    )
```

profile of v0, /device:TPU:0, one launch (start us, length us, event | category | flops | bytes accessed | tf_op | source)
XLA Modules:
  0.0 88.3 jit_solution(16731165367676843982)
XLA Ops:
  0.6 0.0 copy-start
  0.7 0.8 compare_reduce_fusion
  1.5 0.3 reduce-window.9
  1.8 0.1 slice.34
  1.9 0.1 slice_reduce_fusion
  2.1 0.1 add_bitcast_fusion
  2.2 0.3 fusion.9
  2.5 0.7 copy.99
  3.2 7.4 %all-to-all-start = ((bf16[32,16,128]{2,1,0:T(8,128)(2,1)}), bf16[32,16,128]{2,1,0:T(8,128)(2,1)S(1)}, u32[]{:S(2)}, u32[]{:S(2)}) async-start(bf16[32,16,128]{2,1,0:T(8,128)(2,1)} %bitcast.101), calls=%async_computation | async-start | bytes 262144 | tf_op jit(solution)/shard_map/all_to_all | solution.py:52
  10.6 0.7 copy.60
  11.3 0.0 copy-done.3
  11.3 0.2 convolution_convert_fusion.7
  11.5 23.3 %all_gather.3 = bf16[256,1024]{1,0:T(8,128)(2,1)S(1)} all-gather(bf16[16,1024]{1,0:T(8,128)(2,1)S(1)} %convolution_convert_fusion.7), channel_id=1, replica_groups=mesh['groups'=2,'seq'=16] {'seq'}, dimensions={0}, use_global_device_ids=true | all-gather | bytes 557056 | tf_op jit(solution)/shard_map/all_gather | solution.py:59
  34.7 0.0 all-to-all-done
  34.7 3.5 %all-to-all-start.2 = ((bf16[32,16,128]{2,1,0:T(8,128)(2,1)}), bf16[32,16,128]{2,1,0:T(8,128)(2,1)S(1)}, u32[]{:S(2)}, u32[]{:S(2)}) async-start(bf16[32,16,128]{2,1,0:T(8,128)(2,1)} %copy.60), calls=%async_computation.2 | async-start | bytes 262144 | tf_op jit(solution)/shard_map/all_to_all | solution.py:53
  38.3 7.8 %all-to-all-done.2 = bf16[32,16,128]{2,1,0:T(8,128)(2,1)S(1)} async-done(((bf16[32,16,128]{2,1,0:T(8,128)(2,1)}), bf16[32,16,128]{2,1,0:T(8,128)(2,1)S(1)}, u32[]{:S(2)}, u32[]{:S(2)}) %all-to-all-start.2) | async-done | bytes 131104 | tf_op jit(solution)/shard_map/all_to_all | solution.py:53
  46.2 0.1 copy.61
  46.3 0.2 fusion.64
  46.5 0.1 fusion.20
  46.6 0.2 fusion.66
  46.8 0.2 multiply_reduce_fusion.1
  47.1 0.2 fusion.6
  47.3 0.2 fusion.13
  47.5 0.2 fusion.65
  47.7 0.1 copy.62
  47.8 0.2 fusion.63
  48.0 0.1 fusion.22
  48.1 0.2 multiply_reduce_fusion
  48.3 0.2 fusion.7
  48.5 0.2 fusion.12
  48.8 0.8 copy.56
  49.6 3.5 %all-to-all-start.1 = ((bf16[2,256,128]{2,0,1:T(2,128)(2,1)}), bf16[2,256,128]{2,0,1:T(2,128)(2,1)S(1)}, u32[]{:S(2)}, u32[]{:S(2)}) async-start(bf16[2,256,128]{2,0,1:T(2,128)(2,1)} %copy.56), calls=%async_computation.1 | async-start | bytes 262144 | tf_op jit(solution)/shard_map/all_to_all | solution.py:129
  53.1 0.8 copy.63
  53.9 0.2 convolution_add_fusion
  54.1 6.9 %all-to-all-done.1 = bf16[2,256,128]{2,0,1:T(2,128)(2,1)S(1)} async-done(((bf16[2,256,128]{2,0,1:T(2,128)(2,1)}), bf16[2,256,128]{2,0,1:T(2,128)(2,1)S(1)}, u32[]{:S(2)}, u32[]{:S(2)}) %all-to-all-start.1) | async-done | bytes 131104 | tf_op jit(solution)/shard_map/all_to_all | solution.py:129
  61.0 3.5 %all-to-all-start.3 = ((bf16[2,256,128]{2,0,1:T(2,128)(2,1)}), bf16[2,256,128]{2,0,1:T(2,128)(2,1)S(1)}, u32[]{:S(2)}, u32[]{:S(2)}) async-start(bf16[2,256,128]{2,0,1:T(2,128)(2,1)} %copy.63), calls=%async_computation.3 | async-start | bytes 262144 | tf_op jit(solution)/shard_map/all_to_all | solution.py:130
  64.5 0.2 fusion.8
  64.7 0.7 pad_maximum_fusion
  65.4 7.0 %all-to-all-done.3 = bf16[2,256,128]{2,0,1:T(2,128)(2,1)S(1)} async-done(((bf16[2,256,128]{2,0,1:T(2,128)(2,1)}), bf16[2,256,128]{2,0,1:T(2,128)(2,1)S(1)}, u32[]{:S(2)}, u32[]{:S(2)}) %all-to-all-start.3) | async-done | bytes 131104 | tf_op jit(solution)/shard_map/all_to_all | solution.py:130
  72.4 3.5 %all-to-all-start.4 = ((f32[16,16,256]{2,1,0:T(8,128)}), f32[16,16,256]{2,1,0:T(8,128)S(1)}, u32[]{:S(2)}, u32[]{:S(2)}) async-start(f32[16,16,256]{2,1,0:T(8,128)} %bitcast.30), calls=%async_computation.4 | async-start | bytes 524288 | tf_op jit(solution)/shard_map/all_to_all | solution.py:137
  76.0 0.0 copy-start.2
  76.1 0.7 copy.98
  76.8 1.8 %convolution_convert_fusion = bf16[192,4096]{1,0:T(8,128)(2,1)} fusion(bf16[2,8,32,128]{3,2,1,0:T(8,128)(2,1)S(1)} %bitcast.109, s32[192]{0:T(256)S(1)} %add_select_fusion), kind=kOutput, calls=%fused_computation | convolution fusion | flops 25955328 | bytes 1704704 | tf_op jit(solution)/shard_map/dot_general | solution.py:147
  78.6 7.4 %all-to-all-done.4 = f32[16,16,256]{2,1,0:T(8,128)S(1)} async-done(((f32[16,16,256]{2,1,0:T(8,128)}), f32[16,16,256]{2,1,0:T(8,128)S(1)}, u32[]{:S(2)}, u32[]{:S(2)}) %all-to-all-start.4) | async-done | bytes 262176 | tf_op jit(solution)/shard_map/all_to_all | solution.py:137
  86.0 0.0 copy-done.2
  86.0 0.4 fusion.14
  86.4 0.9 %convolution_convert_fusion.3 = bf16[192,512]{1,0:T(8,128)(2,1)} fusion(bf16[2,8,4,128]{3,2,1,0:T(4,128)(2,1)S(1)} %bitcast.127, s32[192]{0:T(256)S(1)} %add_select_fusion), kind=kOutput, calls=%fused_computation.3 | convolution fusion | flops 3247104 | bytes 213760 | tf_op jit(solution)/shard_map/dot_general | solution.py:150
  87.3 0.9 %convolution_convert_fusion.2 = bf16[192,512]{1,0:T(8,128)(2,1)} fusion(bf16[2,8,4,128]{3,2,1,0:T(4,128)(2,1)S(1)} %bitcast.126, s32[192]{0:T(256)S(1)} %add_select_fusion), kind=kOutput, calls=%fused_computation.2 | convolution fusion | flops 3247104 | bytes 213760 | tf_op jit(solution)/shard_map/dot_general | solution.py:151
  (24 shorter events, 0.4 us)
Async XLA Ops:
  0.6 1.5 %copy-start = (bf16[192,4096]{1,0:T(8,128)(2,1)S(1)}, bf16[192,4096]{1,0:T(8,128)(2,1)}, u32[]{:S(2)}) copy-start(bf16[192,4096]{1,0:T(8,128)(2,1)} %param.6) | copy-start | bytes 4718596
  0.6 9.9 %copy-start.1 = (bf16[16,4096]{1,0:T(8,128)(2,1)S(1)}, bf16[16,4096]{1,0:T(8,128)(2,1)}, u32[]{:S(2)}) copy-start(bf16[16,4096]{1,0:T(8,128)(2,1)} %param.10) | copy-start | bytes 393220
  0.7 10.7 %copy-start.3 = (bf16[192,512]{1,0:T(8,128)(2,1)S(1)}, bf16[192,512]{1,0:T(8,128)(2,1)}, u32[]{:S(2)}) copy-start(bf16[192,512]{1,0:T(8,128)(2,1)} %param.8) | copy-start | bytes 589828
  0.7 10.7 %copy-start.4 = (bf16[192,512]{1,0:T(8,128)(2,1)S(1)}, bf16[192,512]{1,0:T(8,128)(2,1)}, u32[]{:S(2)}) copy-start(bf16[192,512]{1,0:T(8,128)(2,1)} %param.7) | copy-start | bytes 589828
  3.2 31.5 %all-to-all-start = ((bf16[32,16,128]{2,1,0:T(8,128)(2,1)}), bf16[32,16,128]{2,1,0:T(8,128)(2,1)S(1)}, u32[]{:S(2)}, u32[]{:S(2)}) async-start(bf16[32,16,128]{2,1,0:T(8,128)(2,1)} %bitcast.101), calls=%async_computation | async-start | bytes 262144 | tf_op jit(solution)/shard_map/all_to_all | solution.py:52
  34.7 11.4 %all-to-all-start.2 = ((bf16[32,16,128]{2,1,0:T(8,128)(2,1)}), bf16[32,16,128]{2,1,0:T(8,128)(2,1)S(1)}, u32[]{:S(2)}, u32[]{:S(2)}) async-start(bf16[32,16,128]{2,1,0:T(8,128)(2,1)} %copy.60), calls=%async_computation.2 | async-start | bytes 262144 | tf_op jit(solution)/shard_map/all_to_all | solution.py:53
  49.6 11.4 %all-to-all-start.1 = ((bf16[2,256,128]{2,0,1:T(2,128)(2,1)}), bf16[2,256,128]{2,0,1:T(2,128)(2,1)S(1)}, u32[]{:S(2)}, u32[]{:S(2)}) async-start(bf16[2,256,128]{2,0,1:T(2,128)(2,1)} %copy.56), calls=%async_computation.1 | async-start | bytes 262144 | tf_op jit(solution)/shard_map/all_to_all | solution.py:129
  61.0 11.4 %all-to-all-start.3 = ((bf16[2,256,128]{2,0,1:T(2,128)(2,1)}), bf16[2,256,128]{2,0,1:T(2,128)(2,1)S(1)}, u32[]{:S(2)}, u32[]{:S(2)}) async-start(bf16[2,256,128]{2,0,1:T(2,128)(2,1)} %copy.63), calls=%async_computation.3 | async-start | bytes 262144 | tf_op jit(solution)/shard_map/all_to_all | solution.py:130
  72.4 13.5 %all-to-all-start.4 = ((f32[16,16,256]{2,1,0:T(8,128)}), f32[16,16,256]{2,1,0:T(8,128)S(1)}, u32[]{:S(2)}, u32[]{:S(2)}) async-start(f32[16,16,256]{2,1,0:T(8,128)} %bitcast.30), calls=%async_computation.4 | async-start | bytes 524288 | tf_op jit(solution)/shard_map/all_to_all | solution.py:137
  76.0 10.0 %copy-start.2 = (f32[16,4,1]{0,1,2:T(4,128)S(1)}, f32[16,4,1]{0,1,2:T(4,128)}, u32[]{:S(2)}) copy-start(f32[16,4,1]{0,1,2:T(4,128)} %constant.157) | copy-start | bytes 772
where the time goes:
time: 88.9 us; the launch traced here: 88.3 us
  waiting for transfers between devices  29.1 us (33%)
  blocking collectives  23.3 us (26%)
  starting transfers between devices  21.4 us (24%)
  matrix products  6.96 us (8%)
  local copies, waits for them, and re-layouts  4.35 us (5%)
  other arithmetic  2.22 us (2%)
  between operations  0.96 us (1%)
    all_gather x1, blocking collectives, body(): gathered = lax.all_gather(kv_kept, 'seq', axis=0, tiled=True)  23.3 us
    all_to_all x1, waiting for transfers between devices, body(): lax.all_to_all(to_units(out_grad, row_parts), 'seq', split_axis=0, concat...  7.84 us
    all_to_all x1, starting transfers between devices, body(): lax.all_to_all(to_units(q_kept, row_parts), 'seq', split_axis=0, concat_a...  7.36 us
    all_to_all x1, waiting for transfers between devices, body(): lax.all_to_all(partial_value, 'seq', split_axis=0, concat_axis=0, tiled=T...  7.35 us
    all_to_all x1, waiting for transfers between devices, body(): lax.all_to_all(jnp.stack(grad_list), 'seq', split_axis=1, concat_axis=0,...  7.01 us
    all_to_all x1, waiting for transfers between devices, body(): lax.all_to_all(jnp.stack(out_list), 'seq', split_axis=1, concat_axis=0, t...  6.9 us
    all_to_all x1, starting transfers between devices, body(): lax.all_to_all(partial_value, 'seq', split_axis=0, concat_axis=0, tiled=T...  3.53 us
    all_to_all x1, starting transfers between devices, body(): lax.all_to_all(to_units(out_grad, row_parts), 'seq', split_axis=0, concat...  3.51 us
  transfers between devices with their start and end apart: 5, of which 4 were waited for; matrix products, arithmetic and copies ran while one was open for 6% of the time, Pallas kernels for 0%

commit v1 on v0

v1 whole, which is shorter than its diff:
```python
import functools

import jax
import jax.numpy as jnp
from jax import lax
from jax.experimental import pallas as pl
from jax.experimental.pallas import tpu as pltpu
from jax.sharding import PartitionSpec as P

HEADS = 32
KVH = 4
HD = 128
GROUP = HEADS // KVH
QUAD = KVH
GW = GROUP * HD
CHUNKS = 2
BF = jnp.bfloat16
F32 = jnp.float32
MESH = pl.DeviceIdType.MESH


def dot(a, b, ca, cb):
    return lax.dot_general(a, b, (((ca,), (cb,)), ((), ())), preferred_element_type=F32)


def kernel(
    n, keep, q_hbm, k_hbm, v_hbm, rank_ref, g_hbm, att_out, dq_out, dk_out, dv_out,
    q_in, k_in, v_in, g_in, q_send, g_send, kv_send, q_recv, g_recv, kv_recv,
    dkv_send, dkv_recv, att_send, dqs_send, att_recv, dqs_recv, dq_full, dk_full, dv_full,
    dk_acc, dv_acc, in_sem, out_sem, qg_ssem, qg_rsem, kv_ssem, kv_rsem,
    ad_ssem, ad_rsem, dkv_ssem, dkv_rsem,
):
    rows = q_in.shape[0]
    me = lax.axis_index("seq")
    quad = me // QUAD
    mine = me % QUAD
    base = quad * QUAD
    keys = n * keep
    scale = HD ** -0.5

    loads = []
    for i, (src, dst) in enumerate(((k_hbm, k_in), (v_hbm, v_in), (g_hbm, g_in), (q_hbm, q_in))):
        cp = pltpu.make_async_copy(src, dst, in_sem.at[i])
        cp.start()
        loads.append(cp)

    barrier = pltpu.get_barrier_semaphore()

    def greet(off, c):
        pl.semaphore_signal(
            barrier, inc=1, device_id={"seq": lax.rem(me + off, n)}, device_id_type=MESH
        )
        return c

    lax.fori_loop(1, n, greet, 0)

    def remote(src, dst, ssem, rsem, target):
        return pltpu.make_async_remote_copy(
            src_ref=src, dst_ref=dst, send_sem=ssem, recv_sem=rsem,
            device_id={"seq": target}, device_id_type=MESH,
        )

    chosen = rank_ref[...] < keep
    chosen_low = jnp.broadcast_to(jnp.where(chosen, 1.0, 0.0).astype(F32), (8, rows)).astype(BF)
    upto = (
        lax.broadcasted_iota(jnp.int32, (rows, rows), 0)
        <= lax.broadcasted_iota(jnp.int32, (rows, rows), 1)
    )
    slots = dot(chosen_low, jnp.where(upto, 1.0, 0.0).astype(BF), 1, 0)[0:1]
    slots = jnp.where(chosen, slots, 0.0)
    wanted = lax.broadcasted_iota(jnp.int32, (keep, rows), 0).astype(F32) + 1.0
    sel = jnp.where(wanted == slots, 1.0, 0.0).astype(BF)

    loads[0].wait()
    loads[1].wait()
    k_kept = dot(sel, k_in[...], 1, 0).astype(BF)
    v_kept = dot(sel, v_in[...], 1, 0).astype(BF)
    for g in range(KVH):
        kv_send[g, :, :HD] = k_kept[:, g * HD:(g + 1) * HD]
        kv_send[g, :, HD:] = v_kept[:, g * HD:(g + 1) * HD]
    kv_recv[me] = kv_send[mine]

    def clear(s, c):
        kv_recv[s] = jnp.zeros((keep, 2 * HD), BF)
        return c

    lax.fori_loop(base + QUAD, n, clear, 0)

    loads[2].wait()
    for h in range(HEADS):
        g_send[h] = g_in[:, h * HD:(h + 1) * HD]

    pl.semaphore_wait(barrier, n - 1)

    def kv_copy(target, source):
        return remote(
            kv_send.at[target % QUAD], kv_recv.at[source], kv_ssem.at[target],
            kv_rsem.at[source], target,
        )

    def qg_copy(which, d, send):
        peer = (mine + d) % QUAD
        buf_s, buf_r = ((q_send, q_recv), (g_send, g_recv))[which]
        return remote(
            buf_s.at[pl.ds(peer * GROUP, GROUP)], buf_r.at[:, mine if send else peer],
            qg_ssem.at[which, d], qg_rsem.at[which, mine if send else peer], base + peer,
        )

    def send_kv(i, c):
        target = n - 1 - i

        @pl.when(target != me)
        def _():
            kv_copy(target, me).start()

        return c

    lax.fori_loop(0, n - base, send_kv, 0)
    for d in (2, 3, 1):
        qg_copy(1, d, True).start()

    loads[3].wait()
    for d in (2, 3, 1, 0):
        peer = (mine + d) % QUAD
        cols = pl.ds(pl.multiple_of(peer * GW, GW), GW)
        part = dot(sel, q_in[:, cols], 1, 0).astype(BF)
        for h in range(GROUP):
            if d == 0:
                q_recv[h, mine] = part[:, h * HD:(h + 1) * HD]
            else:
                q_send[peer * GROUP + h] = part[:, h * HD:(h + 1) * HD]
        if d != 0:
            qg_copy(0, d, True).start()
    for h in range(GROUP):
        g_recv[h, mine] = g_send[mine * GROUP + h]

    def wait_kv(s, c):
        @pl.when(s != me)
        def _():
            kv_copy(s, s).wait_recv()

        return c

    lax.fori_loop(0, base + QUAD, wait_kv, 0)
    for d in (1, 2, 3):
        qg_copy(1, d, False).wait_recv()
    for d in (1, 2, 3):
        qg_copy(0, d, False).wait_recv()

    kv = kv_recv[...].reshape(keys, 2 * HD)
    k_all, v_all = kv[:, :HD], kv[:, HD:]
    span = QUAD * keep
    hc = GROUP // CHUNKS
    crows = hc * span
    row_pos = base * keep + lax.broadcasted_iota(jnp.int32, (crows, keys), 0) % span
    seen = row_pos >= lax.broadcasted_iota(jnp.int32, (crows, keys), 1)

    def ad_copy(which, chunk, d, send):
        peer = (mine + d) % QUAD
        buf_s, buf_r = ((att_send, att_recv), (dqs_send, dqs_recv))[which]
        slot = mine if send else peer
        cols = pl.ds(chunk * hc * HD, hc * HD)
        return remote(
            buf_s.at[peer, :, cols], buf_r.at[slot, :, cols],
            ad_ssem.at[which, chunk, d], ad_rsem.at[which, chunk, slot], base + peer,
        )

    for c in range(CHUNKS):
        q_c = q_recv[c * hc:(c + 1) * hc].reshape(crows, HD)
        g_c = g_recv[c * hc:(c + 1) * hc].reshape(crows, HD)
        scores = jnp.where(seen, dot(q_c, k_all, 1, 1) * scale, -jnp.inf)
        top = jnp.max(scores, axis=1, keepdims=True)
        e = jnp.exp(scores - top)
        probs = e * (1.0 / jnp.sum(e, axis=1, keepdims=True))
        low = probs.astype(BF)
        att = dot(low, v_all, 1, 0).astype(BF)
        gdot = jnp.sum(g_c.astype(F32) * att.astype(F32), axis=1, keepdims=True)
        gprob = dot(g_c, v_all, 1, 1)
        ds = (probs * (gprob - gdot)).astype(BF)
        dq = (dot(ds, k_all, 1, 0) * scale).astype(BF)
        for h in range(hc):
            hcol = slice((c * hc + h) * HD, (c * hc + h + 1) * HD)
            for b in range(QUAD):
                r0 = h * span + b * keep
                att_send[b, :, hcol] = att[r0:r0 + keep]
                dqs_send[b, :, hcol] = dq[r0:r0 + keep]
        for d in (2, 3, 1):
            for w in (0, 1):
                ad_copy(w, c, d, True).start()
        dk_part = dot(ds, q_c, 0, 0)
        dv_part = dot(low, g_c, 0, 0)
        if c == 0:
            dk_acc[...] = dk_part
            dv_acc[...] = dv_part
        else:
            dk_acc[...] += dk_part
            dv_acc[...] += dv_part

    dkv_send[:, :, :HD] = (dk_acc[...] * scale).astype(BF).reshape(n, keep, HD)
    dkv_send[:, :, HD:] = dv_acc[...].astype(BF).reshape(n, keep, HD)

    def dkv_copy(target, source):
        return remote(
            dkv_send.at[target], dkv_recv.at[source], dkv_ssem.at[target],
            dkv_rsem.at[source], target,
        )

    def send_dkv(t, c):
        @pl.when(t != me)
        def _():
            dkv_copy(t, me).start()

        return c

    lax.fori_loop(0, base + QUAD, send_dkv, 0)
    dkv_recv[me] = dkv_send[me]
    att_recv[mine] = att_send[mine]
    dqs_recv[mine] = dqs_send[mine]

    for d in (0, 1, 3, 2):
        peer = (mine + d) % QUAD
        cols = pl.ds(pl.multiple_of(peer * GW, GW), GW)
        if d:
            for c in range(CHUNKS):
                ad_copy(0, c, d, False).wait_recv()
                ad_copy(1, c, d, False).wait_recv()
        pltpu.make_async_copy(att_recv.at[peer], att_out.at[:, cols], out_sem.at[0, d]).start()
        dq_full[:, cols] = dot(sel, dqs_recv[peer], 0, 0).astype(BF)
        pltpu.make_async_copy(dq_full.at[:, cols], dq_out.at[:, cols], out_sem.at[1, d]).start()

    def wait_dkv(s, c):
        @pl.when(s != me)
        def _():
            dkv_copy(s, s).wait_recv()

        return c

    lax.fori_loop(base, n, wait_dkv, 0)

    def add_quad(j, tot):
        return tuple(
            tot[g] + dkv_recv[j * QUAD + g].astype(F32) for g in range(KVH)
        )

    total = lax.fori_loop(
        quad, n // QUAD, add_quad, tuple(jnp.zeros((keep, 2 * HD), F32) for _ in range(KVH))
    )
    dk_kept = jnp.concatenate([t[:, :HD] for t in total], axis=1).astype(BF)
    dv_kept = jnp.concatenate([t[:, HD:] for t in total], axis=1).astype(BF)
    dk_full[...] = dot(sel, dk_kept, 0, 0).astype(BF)
    dv_full[...] = dot(sel, dv_kept, 0, 0).astype(BF)
    last = [
        pltpu.make_async_copy(dk_full, dk_out, out_sem.at[2, 0]),
        pltpu.make_async_copy(dv_full, dv_out, out_sem.at[2, 1]),
    ]
    for cp in last:
        cp.start()

    def drain_kv(t, c):
        @pl.when(t != me)
        def _():
            kv_copy(t, me).wait_send()

        return c

    lax.fori_loop(base, n, drain_kv, 0)

    def drain_dkv(t, c):
        @pl.when(t != me)
        def _():
            dkv_copy(t, me).wait_send()

        return c

    lax.fori_loop(0, base + QUAD, drain_dkv, 0)
    for d in (1, 2, 3):
        for w in (0, 1):
            qg_copy(w, d, True).wait_send()
            for c in range(CHUNKS):
                ad_copy(w, c, d, True).wait_send()
    for d in range(QUAD):
        peer = (mine + d) % QUAD
        cols = pl.ds(pl.multiple_of(peer * GW, GW), GW)
        pltpu.make_async_copy(att_recv.at[peer], att_out.at[:, cols], out_sem.at[0, d]).wait()
        pltpu.make_async_copy(dq_full.at[:, cols], dq_out.at[:, cols], out_sem.at[1, d]).wait()
    for cp in last:
        cp.wait()


def body(query_rows, key_rows, value_rows, keep_rank, out_grad):
    n = lax.axis_size("seq")
    rows = query_rows.shape[0]
    keep = out_grad.shape[0]
    width = HEADS * HD
    kvw = KVH * HD
    any_spec = pl.BlockSpec(memory_space=pl.ANY)
    vmem = pl.BlockSpec(memory_space=pltpu.VMEM)
    dma = pltpu.SemaphoreType.DMA
    return pl.pallas_call(
        functools.partial(kernel, n, keep),
        out_shape=(
            jax.ShapeDtypeStruct((keep, width), BF),
            jax.ShapeDtypeStruct((rows, width), BF),
            jax.ShapeDtypeStruct((rows, kvw), BF),
            jax.ShapeDtypeStruct((rows, kvw), BF),
        ),
        in_specs=[any_spec, any_spec, any_spec, vmem, any_spec],
        out_specs=(any_spec,) * 4,
        scratch_shapes=[
            pltpu.VMEM((rows, width), BF),
            pltpu.VMEM((rows, kvw), BF),
            pltpu.VMEM((rows, kvw), BF),
            pltpu.VMEM((keep, width), BF),
            pltpu.VMEM((HEADS, keep, HD), BF),
            pltpu.VMEM((HEADS, keep, HD), BF),
            pltpu.VMEM((KVH, keep, 2 * HD), BF),
            pltpu.VMEM((GROUP, QUAD, keep, HD), BF),
            pltpu.VMEM((GROUP, QUAD, keep, HD), BF),
            pltpu.VMEM((n, keep, 2 * HD), BF),
            pltpu.VMEM((n, keep, 2 * HD), BF),
            pltpu.VMEM((n, keep, 2 * HD), BF),
            pltpu.VMEM((QUAD, keep, GW), BF),
            pltpu.VMEM((QUAD, keep, GW), BF),
            pltpu.VMEM((QUAD, keep, GW), BF),
            pltpu.VMEM((QUAD, keep, GW), BF),
            pltpu.VMEM((rows, width), BF),
            pltpu.VMEM((rows, kvw), BF),
            pltpu.VMEM((rows, kvw), BF),
            pltpu.VMEM((n * keep, HD), F32),
            pltpu.VMEM((n * keep, HD), F32),
            dma((4,)),
            dma((3, QUAD)),
            dma((2, QUAD)),
            dma((2, QUAD)),
            dma((n,)),
            dma((n,)),
            dma((2, CHUNKS, QUAD)),
            dma((2, CHUNKS, QUAD)),
            dma((n,)),
            dma((n,)),
        ],
        compiler_params=pltpu.CompilerParams(
            collective_id=0, has_side_effects=True, vmem_limit_bytes=48 * 1024 * 1024
        ),
    )(query_rows, key_rows, value_rows, keep_rank, out_grad)


def solution(mesh):
    spec = P(("groups", "seq"), None)
    return jax.shard_map(
        body, mesh=mesh, in_specs=(spec,) * 5, out_specs=(spec,) * 4, check_vma=False
    )
```

time: 88.9 us -> 29.9 us (0.34)
  waiting for transfers between devices: 29.1 us -> 0 us
  blocking collectives: 23.3 us -> 0 us
  starting transfers between devices: 21.4 us -> 0 us
  Pallas kernels: 0 us -> 20.8 us
  matrix products: 6.96 us -> 0 us
  local copies, waits for them, and re-layouts: 4.35 us -> 7.99 us
  other arithmetic: 2.22 us -> 0 us
    all_to_all x5 -> x0, waiting for transfers between devices: 29.1 us -> none  [the longest x1 7.84 us: body(): lax.all_to_all(to_units(out_grad, row_parts), 'seq', split_axis=0, concat...]
    all_gather x1 -> x0, blocking collectives: 23.3 us -> none  [body(): gathered = lax.all_gather(kv_kept, 'seq', axis=0, tiled=True)]
    all_to_all x5 -> x0, starting transfers between devices: 21.4 us -> none  [the longest x1 7.36 us: body(): lax.all_to_all(to_units(q_kept, row_parts), 'seq', split_axis=0, concat_a...]
    pallas_call x0 -> x1, Pallas kernels: none -> 20.8 us  [body(): pl.pallas_call(functools.partial(kernel, n, keep), out_shape=(jax.ShapeDt...]
    unnamed x13 -> x14, local copies, waits for them, and re-layouts: 0.79 us -> 7.99 us
    dot_general x18 -> x0, matrix products: 6.96 us -> none  [the longest x1 1.75 us: body(): jnp.dot(spread, query_kept, preferred_element_type=jnp.float32)]
    another operation x3 -> x0, local copies, waits for them, and re-layouts: 1.69 us -> none  [the longest x1 0.79 us: body(): jnp.stack(grad_list)]
    reshape x2 -> x0, local copies, waits for them, and re-layouts: 1.42 us -> none  [the longest x1 0.71 us: to_units(): shaped = row_block.reshape(kept_count // row_parts, row_parts, HEADS, HD)]
  transfers between devices with their start and end apart: 5 -> 0, of which waited for: 4 -> 0; matrix products, arithmetic and copies ran while one was open for 6% -> 0% of each run, Pallas kernels for 0% -> 0%
where the time goes in v1:
time: 29.9 us; the launch traced here: 29.4 us
  Pallas kernels  20.8 us (70%)
  local copies, waits for them, and re-layouts  7.99 us (27%)
  between operations  0.65 us (2%)
    pallas_call x1, Pallas kernels, body(): pl.pallas_call(functools.partial(kernel, n, keep), out_shape=(jax.ShapeDt...  20.8 us
    unnamed x14, local copies, waits for them, and re-layouts  7.99 us

profile of v1, /device:TPU:0, one launch (start us, length us, event | category | flops | bytes accessed | tf_op | source)
XLA Modules:
  0.0 29.4 jit_solution(12329386602779163067)
XLA Ops:
  0.6 0.0 copy-start
  0.6 1.4 %copy-done = bf16[192,4096]{1,0:T(8,128)(2,1)S(1)} copy-done((bf16[192,4096]{1,0:T(8,128)(2,1)S(1)}, bf16[192,4096]{1,0:T(8,128)(2,1)}, u32[]{:S(2)}) %copy-start) | copy-done | bytes 1572888
  2.0 0.0 copy-start.1
  2.0 0.9 %copy-done.1 = bf16[192,512]{1,0:T(8,128)(2,1)S(1)} copy-done((bf16[192,512]{1,0:T(8,128)(2,1)S(1)}, bf16[192,512]{1,0:T(8,128)(2,1)}, u32[]{:S(2)}) %copy-start.1) | copy-done | bytes 196632
  3.0 0.0 copy-start.2
  3.0 0.9 %copy-done.2 = bf16[192,512]{1,0:T(8,128)(2,1)S(1)} copy-done((bf16[192,512]{1,0:T(8,128)(2,1)S(1)}, bf16[192,512]{1,0:T(8,128)(2,1)}, u32[]{:S(2)}) %copy-start.2) | copy-done | bytes 196632
  3.9 0.0 copy-start.3
  3.9 0.9 %copy-done.3 = bf16[16,4096]{1,0:T(8,128)(2,1)S(1)} copy-done((bf16[16,4096]{1,0:T(8,128)(2,1)S(1)}, bf16[16,4096]{1,0:T(8,128)(2,1)}, u32[]{:S(2)}) %copy-start.3) | copy-done | bytes 131096
  4.8 0.0 copy-start.4
  4.8 0.7 %copy-done.4 = s32[1,192]{1,0:T(1,128)S(1)} copy-done((s32[1,192]{1,0:T(1,128)S(1)}, s32[1,192]{1,0:T(1,128)}, u32[]{:S(2)}) %copy-start.4) | copy-done | bytes 792
  5.5 20.8 %shard_map.84 = (bf16[16,4096]{1,0:T(8,128)(2,1)S(1)}, bf16[192,4096]{1,0:T(8,128)(2,1)S(1)}, bf16[192,512]{1,0:T(8,128)(2,1)S(1)}, bf16[192,512]{1,0:T(8,128)(2,1)S(1)}) custom-call(bf16[192,4096]{1,0:T(8,128)(2,1)S(1)} %copy-done, bf16[192,512]{1,0:T(8,128)(2,1)S(1)} %copy-done.1, bf16[192,512]{1,0:T(8,128)(2,1)S(1)} %copy-done.2, s32[1,192]{1,0:T(1,128)S(1)} %copy-done.4, ...), custom_call_target="tpu_custom_call" | custom-call | tf_op jit(solution)/shard_map/pallas_call | solution.py:299
  26.3 0.7 %copy.13 = bf16[16,4096]{1,0:T(8,128)(2,1)} copy(bf16[16,4096]{1,0:T(8,128)(2,1)S(1)} %get-tuple-element.8) | data formatting | bytes 262144
  26.9 1.1 %copy.14 = bf16[192,4096]{1,0:T(8,128)(2,1)} copy(bf16[192,4096]{1,0:T(8,128)(2,1)S(1)} %get-tuple-element.9) | data formatting | bytes 3145728
  28.1 0.7 %copy.15 = bf16[192,512]{1,0:T(8,128)(2,1)} copy(bf16[192,512]{1,0:T(8,128)(2,1)S(1)} %get-tuple-element.10) | data formatting | bytes 393216
  28.8 0.7 %copy.16 = bf16[192,512]{1,0:T(8,128)(2,1)} copy(bf16[192,512]{1,0:T(8,128)(2,1)S(1)} %get-tuple-element.11) | data formatting | bytes 393216
Async XLA Ops:
  0.6 1.4 %copy-start = (bf16[192,4096]{1,0:T(8,128)(2,1)S(1)}, bf16[192,4096]{1,0:T(8,128)(2,1)}, u32[]{:S(2)}) copy-start(bf16[192,4096]{1,0:T(8,128)(2,1)} %q_hbm.1) | copy-start | bytes 4718596
  2.0 0.9 %copy-start.1 = (bf16[192,512]{1,0:T(8,128)(2,1)S(1)}, bf16[192,512]{1,0:T(8,128)(2,1)}, u32[]{:S(2)}) copy-start(bf16[192,512]{1,0:T(8,128)(2,1)} %k_hbm.1) | copy-start | bytes 589828
  3.0 0.9 %copy-start.2 = (bf16[192,512]{1,0:T(8,128)(2,1)S(1)}, bf16[192,512]{1,0:T(8,128)(2,1)}, u32[]{:S(2)}) copy-start(bf16[192,512]{1,0:T(8,128)(2,1)} %v_hbm.1) | copy-start | bytes 589828
  3.9 0.9 %copy-start.3 = (bf16[16,4096]{1,0:T(8,128)(2,1)S(1)}, bf16[16,4096]{1,0:T(8,128)(2,1)}, u32[]{:S(2)}) copy-start(bf16[16,4096]{1,0:T(8,128)(2,1)} %g_hbm.1) | copy-start | bytes 393220
  4.8 0.7 %copy-start.4 = (s32[1,192]{1,0:T(1,128)S(1)}, s32[1,192]{1,0:T(1,128)}, u32[]{:S(2)}) copy-start(s32[1,192]{1,0:T(1,128)} %rank_ref.1) | copy-start | bytes 2308

commit v2 on v1

--- a/solution.py
+++ b/solution.py
@@ -24,9 +24,9 @@
 
 
 def kernel(
-    n, keep, q_hbm, k_hbm, v_hbm, rank_ref, g_hbm, att_out, dq_out, dk_out, dv_out,
+    n, keep, q_hbm, k_hbm, v_hbm, rank_ref, g_hbm, att_out, dq_out, dkv_out, sel_out,
     q_in, k_in, v_in, g_in, q_send, g_send, kv_send, q_recv, g_recv, kv_recv,
-    dkv_send, dkv_recv, att_send, dqs_send, att_recv, dqs_recv, dq_full, dk_full, dv_full,
+    dkv_send, dkv_recv, att_send, dqs_send, att_recv, dqs_recv, dkv_kept, sel_keep,
     dk_acc, dv_acc, in_sem, out_sem, qg_ssem, qg_rsem, kv_ssem, kv_rsem,
     ad_ssem, ad_rsem, dkv_ssem, dkv_rsem,
 ):
@@ -70,6 +70,9 @@
     slots = jnp.where(chosen, slots, 0.0)
     wanted = lax.broadcasted_iota(jnp.int32, (keep, rows), 0).astype(F32) + 1.0
     sel = jnp.where(wanted == slots, 1.0, 0.0).astype(BF)
+    sel_keep[...] = sel
+    sel_copy = pltpu.make_async_copy(sel_keep, sel_out, out_sem.at[2, 0])
+    sel_copy.start()
 
     loads[0].wait()
     loads[1].wait()
@@ -225,8 +228,7 @@
                 ad_copy(0, c, d, False).wait_recv()
                 ad_copy(1, c, d, False).wait_recv()
         pltpu.make_async_copy(att_recv.at[peer], att_out.at[:, cols], out_sem.at[0, d]).start()
-        dq_full[:, cols] = dot(sel, dqs_recv[peer], 0, 0).astype(BF)
-        pltpu.make_async_copy(dq_full.at[:, cols], dq_out.at[:, cols], out_sem.at[1, d]).start()
+        pltpu.make_async_copy(dqs_recv.at[peer], dq_out.at[:, cols], out_sem.at[1, d]).start()
 
     def wait_dkv(s, c):
         @pl.when(s != me)
@@ -245,16 +247,11 @@
     total = lax.fori_loop(
         quad, n // QUAD, add_quad, tuple(jnp.zeros((keep, 2 * HD), F32) for _ in range(KVH))
     )
-    dk_kept = jnp.concatenate([t[:, :HD] for t in total], axis=1).astype(BF)
-    dv_kept = jnp.concatenate([t[:, HD:] for t in total], axis=1).astype(BF)
-    dk_full[...] = dot(sel, dk_kept, 0, 0).astype(BF)
-    dv_full[...] = dot(sel, dv_kept, 0, 0).astype(BF)
-    last = [
-        pltpu.make_async_copy(dk_full, dk_out, out_sem.at[2, 0]),
-        pltpu.make_async_copy(dv_full, dv_out, out_sem.at[2, 1]),
-    ]
-    for cp in last:
-        cp.start()
+    for g in range(KVH):
+        dkv_kept[:, g * HD:(g + 1) * HD] = total[g][:, :HD].astype(BF)
+        dkv_kept[:, (KVH + g) * HD:(KVH + g + 1) * HD] = total[g][:, HD:].astype(BF)
+    last = [sel_copy, pltpu.make_async_copy(dkv_kept, dkv_out, out_sem.at[2, 1])]
+    last[1].start()
 
     def drain_kv(t, c):
         @pl.when(t != me)
@@ -282,8 +279,39 @@
         peer = (mine + d) % QUAD
         cols = pl.ds(pl.multiple_of(peer * GW, GW), GW)
         pltpu.make_async_copy(att_recv.at[peer], att_out.at[:, cols], out_sem.at[0, d]).wait()
-        pltpu.make_async_copy(dq_full.at[:, cols], dq_out.at[:, cols], out_sem.at[1, d]).wait()
+        pltpu.make_async_copy(dqs_recv.at[peer], dq_out.at[:, cols], out_sem.at[1, d]).wait()
     for cp in last:
+        cp.wait()
+
+
+def spread_kernel(
+    att_in, dq_in, dkv_in, sel_in, att_out, dq_out, dk_out, dv_out,
+    dq_kept, dkv_kept, sel_ref, dq_full, dk_full, dv_full, in_sem, out_sem,
+):
+    kvw = KVH * HD
+    loads = []
+    for i, (src, dst) in enumerate(
+        ((sel_in, sel_ref), (dq_in, dq_kept), (dkv_in, dkv_kept), (att_in, att_out))
+    ):
+        cp = pltpu.make_async_copy(src, dst, in_sem.at[i])
+        cp.start()
+        loads.append(cp)
+    loads[0].wait()
+    loads[1].wait()
+    sel = sel_ref[...]
+    stores = []
+    for i in range(QUAD):
+        cols = slice(i * GW, (i + 1) * GW)
+        dq_full[:, cols] = dot(sel, dq_kept[:, cols], 0, 0).astype(BF)
+        stores.append(pltpu.make_async_copy(dq_full.at[:, cols], dq_out.at[:, cols], out_sem.at[i]))
+        stores[-1].start()
+    loads[2].wait()
+    for i, (full, out) in enumerate(((dk_full, dk_out), (dv_full, dv_out))):
+        full[...] = dot(sel, dkv_kept[:, i * kvw:(i + 1) * kvw], 0, 0).astype(BF)
+        stores.append(pltpu.make_async_copy(full, out, out_sem.at[QUAD + i]))
+        stores[-1].start()
+    loads[3].wait()
+    for cp in stores:
         cp.wait()
 
 
@@ -296,15 +324,16 @@
     any_spec = pl.BlockSpec(memory_space=pl.ANY)
     vmem = pl.BlockSpec(memory_space=pltpu.VMEM)
     dma = pltpu.SemaphoreType.DMA
-    return pl.pallas_call(
+    hbm = pl.BlockSpec(memory_space=pltpu.HBM)
+    att, dq_kept, dkv_kept, sel = pl.pallas_call(
         functools.partial(kernel, n, keep),
         out_shape=(
             jax.ShapeDtypeStruct((keep, width), BF),
-            jax.ShapeDtypeStruct((rows, width), BF),
-            jax.ShapeDtypeStruct((rows, kvw), BF),
-            jax.ShapeDtypeStruct((rows, kvw), BF),
+            jax.ShapeDtypeStruct((keep, width), BF),
+            jax.ShapeDtypeStruct((keep, 2 * kvw), BF),
+            jax.ShapeDtypeStruct((keep, rows), BF),
         ),
-        in_specs=[any_spec, any_spec, any_spec, vmem, any_spec],
+        in_specs=[hbm, hbm, hbm, vmem, hbm],
         out_specs=(any_spec,) * 4,
         scratch_shapes=[
             pltpu.VMEM((rows, width), BF),
@@ -323,9 +352,8 @@
             pltpu.VMEM((QUAD, keep, GW), BF),
             pltpu.VMEM((QUAD, keep, GW), BF),
             pltpu.VMEM((QUAD, keep, GW), BF),
-            pltpu.VMEM((rows, width), BF),
-            pltpu.VMEM((rows, kvw), BF),
-            pltpu.VMEM((rows, kvw), BF),
+            pltpu.VMEM((keep, 2 * kvw), BF),
+            pltpu.VMEM((keep, rows), BF),
             pltpu.VMEM((n * keep, HD), F32),
             pltpu.VMEM((n * keep, HD), F32),
             dma((4,)),
@@ -340,9 +368,31 @@
             dma((n,)),
         ],
         compiler_params=pltpu.CompilerParams(
-            collective_id=0, has_side_effects=True, vmem_limit_bytes=48 * 1024 * 1024
+            collective_id=0, has_side_effects=True, vmem_limit_bytes=64 * 1024 * 1024
         ),
     )(query_rows, key_rows, value_rows, keep_rank, out_grad)
+    return pl.pallas_call(
+        spread_kernel,
+        out_shape=(
+            jax.ShapeDtypeStruct((keep, width), BF),
+            jax.ShapeDtypeStruct((rows, width), BF),
+            jax.ShapeDtypeStruct((rows, kvw), BF),
+            jax.ShapeDtypeStruct((rows, kvw), BF),
+        ),
+        in_specs=[any_spec] * 4,
+        out_specs=(hbm,) * 4,
+        scratch_shapes=[
+            pltpu.VMEM((keep, width), BF),
+            pltpu.VMEM((keep, 2 * kvw), BF),
+            pltpu.VMEM((keep, rows), BF),
+            pltpu.VMEM((rows, width), BF),
+            pltpu.VMEM((rows, kvw), BF),
+            pltpu.VMEM((rows, kvw), BF),
+            dma((4,)),
+            dma((QUAD + 2,)),
+        ],
+        compiler_params=pltpu.CompilerParams(vmem_limit_bytes=64 * 1024 * 1024),
+    )(att, dq_kept, dkv_kept, sel)
 
 
 def solution(mesh):

time: 29.9 us -> 26.3 us (0.88)
  local copies, waits for them, and re-layouts: 7.99 us -> 0 us
  Pallas kernels: 20.8 us -> 25.4 us
    unnamed x14 -> x0, local copies, waits for them, and re-layouts: 7.99 us -> none
    pallas_call x0 -> x1, Pallas kernels: none -> 5.17 us  [body(): pl.pallas_call(spread_kernel, out_shape=(jax.ShapeDtypeStruct((keep, widt...]
    pallas_call x1, Pallas kernels: 20.8 us -> 20.3 us  [body(): pl.pallas_call(functools.partial(kernel, n, keep), out_shape=(jax.ShapeDt...]
where the time goes in v2:
time: 26.3 us; the launch traced here: 26.1 us
  Pallas kernels  25.4 us (97%)
  between operations  0.64 us (2%)
    pallas_call x1, Pallas kernels, body(): pl.pallas_call(functools.partial(kernel, n, keep), out_shape=(jax.ShapeDt...  20.3 us
    pallas_call x1, Pallas kernels, body(): pl.pallas_call(spread_kernel, out_shape=(jax.ShapeDtypeStruct((keep, widt...  5.17 us

profile of v2, /device:TPU:0, one launch (start us, length us, event | category | flops | bytes accessed | tf_op | source)
XLA Modules:
  0.0 26.1 jit_solution(803094896204357621)
XLA Ops:
  0.6 20.3 %shard_map.84 = (bf16[16,4096]{1,0:T(8,128)(2,1)}, bf16[16,4096]{1,0:T(8,128)(2,1)}, bf16[16,1024]{1,0:T(8,128)(2,1)}, bf16[16,192]{1,0:T(8,128)(2,1)}) custom-call(bf16[192,4096]{1,0:T(8,128)(2,1)} %q_hbm.1, bf16[192,512]{1,0:T(8,128)(2,1)} %k_hbm.1, bf16[192,512]{1,0:T(8,128)(2,1)} %v_hbm.1, s32[1,192]{1,0:T(1,128)} %rank_ref.1, bf16[16,4096]{1,0:T(8,128)(2,1)} %g_hbm.1), custom_call_target="tpu_custom_call" | custom-call | tf_op jit(solution)/shard_map/pallas_call | solution.py:328
  20.9 5.2 %shard_map.85 = (bf16[16,4096]{1,0:T(8,128)(2,1)}, bf16[192,4096]{1,0:T(8,128)(2,1)}, bf16[192,512]{1,0:T(8,128)(2,1)}, bf16[192,512]{1,0:T(8,128)(2,1)}) custom-call(bf16[16,4096]{1,0:T(8,128)(2,1)} %get-tuple-element.8.att_in, bf16[16,4096]{1,0:T(8,128)(2,1)} %get-tuple-element.9.dq_in, bf16[16,1024]{1,0:T(8,128)(2,1)} %get-tuple-element.10.dkv_in, ...), custom_call_target="tpu_custom_call" | custom-call | tf_op jit(solution)/shard_map/pallas_call | solution.py:374

commit v3 on v2

--- a/solution.py
+++ b/solution.py
@@ -37,6 +37,11 @@
     base = quad * QUAD
     keys = n * keep
     scale = HD ** -0.5
+    hc = GROUP // CHUNKS
+    span = QUAD * keep
+
+    def peer_of(d):
+        return (mine // 2 + d // 2) % 2 * 2 + (mine + d) % 2
 
     loads = []
     for i, (src, dst) in enumerate(((k_hbm, k_in), (v_hbm, v_in), (g_hbm, g_in), (q_hbm, q_in))):
@@ -101,12 +106,13 @@
             kv_rsem.at[source], target,
         )
 
-    def qg_copy(which, d, send):
-        peer = (mine + d) % QUAD
+    def qg_copy(which, c, d, send):
+        peer = peer_of(d)
         buf_s, buf_r = ((q_send, q_recv), (g_send, g_recv))[which]
         return remote(
-            buf_s.at[pl.ds(peer * GROUP, GROUP)], buf_r.at[:, mine if send else peer],
-            qg_ssem.at[which, d], qg_rsem.at[which, mine if send else peer], base + peer,
+            buf_s.at[pl.ds(peer * GROUP + c * hc, hc)],
+            buf_r.at[pl.ds(c * hc, hc), mine if send else peer],
+            qg_ssem.at[which, c, d], qg_rsem.at[which, c, mine if send else peer], base + peer,
         )
 
     def send_kv(i, c):
@@ -120,20 +126,24 @@
 
     lax.fori_loop(0, n - base, send_kv, 0)
     for d in (2, 3, 1):
-        qg_copy(1, d, True).start()
+        qg_copy(1, 0, d, True).start()
 
     loads[3].wait()
-    for d in (2, 3, 1, 0):
-        peer = (mine + d) % QUAD
-        cols = pl.ds(pl.multiple_of(peer * GW, GW), GW)
-        part = dot(sel, q_in[:, cols], 1, 0).astype(BF)
-        for h in range(GROUP):
-            if d == 0:
-                q_recv[h, mine] = part[:, h * HD:(h + 1) * HD]
-            else:
-                q_send[peer * GROUP + h] = part[:, h * HD:(h + 1) * HD]
-        if d != 0:
-            qg_copy(0, d, True).start()
+    for c in range(CHUNKS):
+        for d in (2, 3, 1, 0):
+            peer = peer_of(d)
+            cols = pl.ds(pl.multiple_of(peer * GW + c * hc * HD, hc * HD), hc * HD)
+            part = dot(sel, q_in[:, cols], 1, 0).astype(BF)
+            for h in range(hc):
+                piece = part[:, h * HD:(h + 1) * HD]
+                if d == 0:
+                    q_recv[c * hc + h, mine] = piece
+                else:
+                    q_send[peer * GROUP + c * hc + h] = piece
+            if d != 0:
+                qg_copy(0, c, d, True).start()
+                if c + 1 < CHUNKS:
+                    qg_copy(1, c + 1, d, True).start()
     for h in range(GROUP):
         g_recv[h, mine] = g_send[mine * GROUP + h]
 
@@ -145,21 +155,28 @@
         return c
 
     lax.fori_loop(0, base + QUAD, wait_kv, 0)
-    for d in (1, 2, 3):
-        qg_copy(1, d, False).wait_recv()
-    for d in (1, 2, 3):
-        qg_copy(0, d, False).wait_recv()
 
     kv = kv_recv[...].reshape(keys, 2 * HD)
     k_all, v_all = kv[:, :HD], kv[:, HD:]
-    span = QUAD * keep
-    hc = GROUP // CHUNKS
     crows = hc * span
     row_pos = base * keep + lax.broadcasted_iota(jnp.int32, (crows, keys), 0) % span
     seen = row_pos >= lax.broadcasted_iota(jnp.int32, (crows, keys), 1)
 
+    def dkv_copy(target, source):
+        return remote(
+            dkv_send.at[target], dkv_recv.at[source], dkv_ssem.at[target],
+            dkv_rsem.at[source], target,
+        )
+
+    def send_dkv(t, c):
+        @pl.when(t != me)
+        def _():
+            dkv_copy(t, me).start()
+
+        return c
+
     def ad_copy(which, chunk, d, send):
-        peer = (mine + d) % QUAD
+        peer = peer_of(d)
         buf_s, buf_r = ((att_send, att_recv), (dqs_send, dqs_recv))[which]
         slot = mine if send else peer
         cols = pl.ds(chunk * hc * HD, hc * HD)
@@ -169,6 +186,9 @@
         )
 
     for c in range(CHUNKS):
+        for d in (1, 2, 3):
+            qg_copy(1, c, d, False).wait_recv()
+            qg_copy(0, c, d, False).wait_recv()
         q_c = q_recv[c * hc:(c + 1) * hc].reshape(crows, HD)
         g_c = g_recv[c * hc:(c + 1) * hc].reshape(crows, HD)
         scores = jnp.where(seen, dot(q_c, k_all, 1, 1) * scale, -jnp.inf)
@@ -180,48 +200,39 @@
         gdot = jnp.sum(g_c.astype(F32) * att.astype(F32), axis=1, keepdims=True)
         gprob = dot(g_c, v_all, 1, 1)
         ds = (probs * (gprob - gdot)).astype(BF)
-        dq = (dot(ds, k_all, 1, 0) * scale).astype(BF)
-        for h in range(hc):
-            hcol = slice((c * hc + h) * HD, (c * hc + h + 1) * HD)
-            for b in range(QUAD):
-                r0 = h * span + b * keep
-                att_send[b, :, hcol] = att[r0:r0 + keep]
-                dqs_send[b, :, hcol] = dq[r0:r0 + keep]
-        for d in (2, 3, 1):
-            for w in (0, 1):
-                ad_copy(w, c, d, True).start()
+        def give(which, val):
+            buf = (att_send, dqs_send)[which]
+            for h in range(hc):
+                hcol = slice((c * hc + h) * HD, (c * hc + h + 1) * HD)
+                for b in range(QUAD):
+                    r0 = h * span + b * keep
+                    buf[b, :, hcol] = val[r0:r0 + keep]
+            for d in (2, 3, 1):
+                ad_copy(which, c, d, True).start()
+
+        give(0, att)
+        if c < CHUNKS - 1:
+            give(1, (dot(ds, k_all, 1, 0) * scale).astype(BF))
         dk_part = dot(ds, q_c, 0, 0)
         dv_part = dot(low, g_c, 0, 0)
-        if c == 0:
+        if c:
+            dk_part += dk_acc[...]
+            dv_part += dv_acc[...]
+        if c < CHUNKS - 1:
             dk_acc[...] = dk_part
             dv_acc[...] = dv_part
         else:
-            dk_acc[...] += dk_part
-            dv_acc[...] += dv_part
-
-    dkv_send[:, :, :HD] = (dk_acc[...] * scale).astype(BF).reshape(n, keep, HD)
-    dkv_send[:, :, HD:] = dv_acc[...].astype(BF).reshape(n, keep, HD)
-
-    def dkv_copy(target, source):
-        return remote(
-            dkv_send.at[target], dkv_recv.at[source], dkv_ssem.at[target],
-            dkv_rsem.at[source], target,
-        )
-
-    def send_dkv(t, c):
-        @pl.when(t != me)
-        def _():
-            dkv_copy(t, me).start()
-
-        return c
-
-    lax.fori_loop(0, base + QUAD, send_dkv, 0)
+            dkv_send[:, :, :HD] = (dk_part * scale).astype(BF).reshape(n, keep, HD)
+            dkv_send[:, :, HD:] = dv_part.astype(BF).reshape(n, keep, HD)
+            lax.fori_loop(0, base + QUAD, send_dkv, 0)
+            give(1, (dot(ds, k_all, 1, 0) * scale).astype(BF))
+
     dkv_recv[me] = dkv_send[me]
     att_recv[mine] = att_send[mine]
     dqs_recv[mine] = dqs_send[mine]
 
     for d in (0, 1, 3, 2):
-        peer = (mine + d) % QUAD
+        peer = peer_of(d)
         cols = pl.ds(pl.multiple_of(peer * GW, GW), GW)
         if d:
             for c in range(CHUNKS):
@@ -272,11 +283,11 @@
     lax.fori_loop(0, base + QUAD, drain_dkv, 0)
     for d in (1, 2, 3):
         for w in (0, 1):
-            qg_copy(w, d, True).wait_send()
             for c in range(CHUNKS):
+                qg_copy(w, c, d, True).wait_send()
                 ad_copy(w, c, d, True).wait_send()
     for d in range(QUAD):
-        peer = (mine + d) % QUAD
+        peer = peer_of(d)
         cols = pl.ds(pl.multiple_of(peer * GW, GW), GW)
         pltpu.make_async_copy(att_recv.at[peer], att_out.at[:, cols], out_sem.at[0, d]).wait()
         pltpu.make_async_copy(dqs_recv.at[peer], dq_out.at[:, cols], out_sem.at[1, d]).wait()
@@ -286,12 +297,12 @@
 
 def spread_kernel(
     att_in, dq_in, dkv_in, sel_in, att_out, dq_out, dk_out, dv_out,
-    dq_kept, dkv_kept, sel_ref, dq_full, dk_full, dv_full, in_sem, out_sem,
+    dq_kept, dkv_kept, sel_ref, dq_full, dk_full, dv_full, att_keep, in_sem, out_sem,
 ):
     kvw = KVH * HD
     loads = []
     for i, (src, dst) in enumerate(
-        ((sel_in, sel_ref), (dq_in, dq_kept), (dkv_in, dkv_kept), (att_in, att_out))
+        ((sel_in, sel_ref), (dq_in, dq_kept), (dkv_in, dkv_kept), (att_in, att_keep))
     ):
         cp = pltpu.make_async_copy(src, dst, in_sem.at[i])
         cp.start()
@@ -311,6 +322,8 @@
         stores.append(pltpu.make_async_copy(full, out, out_sem.at[QUAD + i]))
         stores[-1].start()
     loads[3].wait()
+    stores.append(pltpu.make_async_copy(att_keep, att_out, out_sem.at[QUAD + 2]))
+    stores[-1].start()
     for cp in stores:
         cp.wait()
 
@@ -358,8 +371,8 @@
             pltpu.VMEM((n * keep, HD), F32),
             dma((4,)),
             dma((3, QUAD)),
-            dma((2, QUAD)),
-            dma((2, QUAD)),
+            dma((2, CHUNKS, QUAD)),
+            dma((2, CHUNKS, QUAD)),
             dma((n,)),
             dma((n,)),
             dma((2, CHUNKS, QUAD)),
@@ -388,8 +401,9 @@
             pltpu.VMEM((rows, width), BF),
             pltpu.VMEM((rows, kvw), BF),
             pltpu.VMEM((rows, kvw), BF),
+            pltpu.VMEM((keep, width), BF),
             dma((4,)),
-            dma((QUAD + 2,)),
+            dma((QUAD + 3,)),
         ],
         compiler_params=pltpu.CompilerParams(vmem_limit_bytes=64 * 1024 * 1024),
     )(att, dq_kept, dkv_kept, sel)

time: 26.3 us -> 23.4 us (0.89)
  Pallas kernels: 25.4 us -> 22.6 us
    pallas_call x1, Pallas kernels: 5.17 us -> 2.6 us  [body(): pl.pallas_call(spread_kernel, out_shape=(jax.ShapeDtypeStruct((keep, widt...]
    pallas_call x1, Pallas kernels: 20.3 us -> 20 us  [body(): pl.pallas_call(functools.partial(kernel, n, keep), out_shape=(jax.ShapeDt...]
where the time goes in v3:
time: 23.4 us; the launch traced here: 23.2 us
  Pallas kernels  22.6 us (97%)
  between operations  0.64 us (3%)
    pallas_call x1, Pallas kernels, body(): pl.pallas_call(functools.partial(kernel, n, keep), out_shape=(jax.ShapeDt...  20 us
    pallas_call x1, Pallas kernels, body(): pl.pallas_call(spread_kernel, out_shape=(jax.ShapeDtypeStruct((keep, widt...  2.6 us

profile of v3, /device:TPU:0, one launch (start us, length us, event | category | flops | bytes accessed | tf_op | source)
XLA Modules:
  0.0 23.2 jit_solution(10080437201536945437)
XLA Ops:
  0.6 20.0 %shard_map.84 = (bf16[16,4096]{1,0:T(8,128)(2,1)}, bf16[16,4096]{1,0:T(8,128)(2,1)}, bf16[16,1024]{1,0:T(8,128)(2,1)}, bf16[16,192]{1,0:T(8,128)(2,1)}) custom-call(bf16[192,4096]{1,0:T(8,128)(2,1)} %q_hbm.1, bf16[192,512]{1,0:T(8,128)(2,1)} %k_hbm.1, bf16[192,512]{1,0:T(8,128)(2,1)} %v_hbm.1, s32[1,192]{1,0:T(1,128)} %rank_ref.1, bf16[16,4096]{1,0:T(8,128)(2,1)} %g_hbm.1), custom_call_target="tpu_custom_call" | custom-call | tf_op jit(solution)/shard_map/pallas_call | solution.py:341
  20.6 2.6 %shard_map.85 = (bf16[16,4096]{1,0:T(8,128)(2,1)}, bf16[192,4096]{1,0:T(8,128)(2,1)}, bf16[192,512]{1,0:T(8,128)(2,1)}, bf16[192,512]{1,0:T(8,128)(2,1)}) custom-call(bf16[16,4096]{1,0:T(8,128)(2,1)} %get-tuple-element.8.att_in, bf16[16,4096]{1,0:T(8,128)(2,1)} %get-tuple-element.9.dq_in, bf16[16,1024]{1,0:T(8,128)(2,1)} %get-tuple-element.10.dkv_in, ...), custom_call_target="tpu_custom_call" | custom-call | tf_op jit(solution)/shard_map/pallas_call | solution.py:387

commit v4 on v3

--- a/solution.py
+++ b/solution.py
@@ -43,21 +43,21 @@
     def peer_of(d):
         return (mine // 2 + d // 2) % 2 * 2 + (mine + d) % 2
 
+    barrier = pltpu.get_barrier_semaphore()
+
+    def greet(off, c):
+        pl.semaphore_signal(
+            barrier, inc=1, device_id={"seq": lax.rem(me + off, n)}, device_id_type=MESH
+        )
+        return c
+
+    lax.fori_loop(1, n, greet, 0)
+
     loads = []
     for i, (src, dst) in enumerate(((k_hbm, k_in), (v_hbm, v_in), (g_hbm, g_in), (q_hbm, q_in))):
         cp = pltpu.make_async_copy(src, dst, in_sem.at[i])
         cp.start()
         loads.append(cp)
-
-    barrier = pltpu.get_barrier_semaphore()
-
-    def greet(off, c):
-        pl.semaphore_signal(
-            barrier, inc=1, device_id={"seq": lax.rem(me + off, n)}, device_id_type=MESH
-        )
-        return c
-
-    lax.fori_loop(1, n, greet, 0)
 
     def remote(src, dst, ssem, rsem, target):
         return pltpu.make_async_remote_copy(
@@ -124,9 +124,9 @@
 
         return c
 
-    lax.fori_loop(0, n - base, send_kv, 0)
     for d in (2, 3, 1):
         qg_copy(1, 0, d, True).start()
+    lax.fori_loop(0, n - base, send_kv, 0)
 
     loads[3].wait()
     for c in range(CHUNKS):
@@ -248,9 +248,8 @@
 
         return c
 
-    lax.fori_loop(base, n, wait_dkv, 0)
-
     def add_quad(j, tot):
+        lax.fori_loop(j * QUAD, j * QUAD + QUAD, wait_dkv, 0)
         return tuple(
             tot[g] + dkv_recv[j * QUAD + g].astype(F32) for g in range(KVH)
         )

time: 23.4 us -> 23.4 us (level)
  no operation moved by 1% of the time
where the time goes in v4:
time: 23.4 us; the launch traced here: 23.2 us
  Pallas kernels  22.6 us (97%)
  between operations  0.64 us (3%)
    pallas_call x1, Pallas kernels, body(): pl.pallas_call(functools.partial(kernel, n, keep), out_shape=(jax.ShapeDt...  20 us
    pallas_call x1, Pallas kernels, body(): pl.pallas_call(spread_kernel, out_shape=(jax.ShapeDtypeStruct((keep, widt...  2.61 us

profile of v4, /device:TPU:0, one launch (start us, length us, event | category | flops | bytes accessed | tf_op | source)
XLA Modules:
  0.0 23.2 jit_solution(5612021446710091203)
XLA Ops:
  0.6 20.0 %shard_map.84 = (bf16[16,4096]{1,0:T(8,128)(2,1)}, bf16[16,4096]{1,0:T(8,128)(2,1)}, bf16[16,1024]{1,0:T(8,128)(2,1)}, bf16[16,192]{1,0:T(8,128)(2,1)}) custom-call(bf16[192,4096]{1,0:T(8,128)(2,1)} %q_hbm.1, bf16[192,512]{1,0:T(8,128)(2,1)} %k_hbm.1, bf16[192,512]{1,0:T(8,128)(2,1)} %v_hbm.1, s32[1,192]{1,0:T(1,128)} %rank_ref.1, bf16[16,4096]{1,0:T(8,128)(2,1)} %g_hbm.1), custom_call_target="tpu_custom_call" | custom-call | tf_op jit(solution)/shard_map/pallas_call | solution.py:340
  20.6 2.6 %shard_map.85 = (bf16[16,4096]{1,0:T(8,128)(2,1)}, bf16[192,4096]{1,0:T(8,128)(2,1)}, bf16[192,512]{1,0:T(8,128)(2,1)}, bf16[192,512]{1,0:T(8,128)(2,1)}) custom-call(bf16[16,4096]{1,0:T(8,128)(2,1)} %get-tuple-element.8.att_in, bf16[16,4096]{1,0:T(8,128)(2,1)} %get-tuple-element.9.dq_in, bf16[16,1024]{1,0:T(8,128)(2,1)} %get-tuple-element.10.dkv_in, ...), custom_call_target="tpu_custom_call" | custom-call | tf_op jit(solution)/shard_map/pallas_call | solution.py:386

commit v5 on v4

--- a/solution.py
+++ b/solution.py
@@ -14,6 +14,8 @@
 QUAD = KVH
 GW = GROUP * HD
 CHUNKS = 2
+PIECES = 8
+PW = HEADS * HD // PIECES
 BF = jnp.bfloat16
 F32 = jnp.float32
 MESH = pl.DeviceIdType.MESH
@@ -310,18 +312,18 @@
     loads[1].wait()
     sel = sel_ref[...]
     stores = []
-    for i in range(QUAD):
-        cols = slice(i * GW, (i + 1) * GW)
+    for i in range(PIECES):
+        cols = slice(i * PW, (i + 1) * PW)
         dq_full[:, cols] = dot(sel, dq_kept[:, cols], 0, 0).astype(BF)
         stores.append(pltpu.make_async_copy(dq_full.at[:, cols], dq_out.at[:, cols], out_sem.at[i]))
         stores[-1].start()
     loads[2].wait()
     for i, (full, out) in enumerate(((dk_full, dk_out), (dv_full, dv_out))):
         full[...] = dot(sel, dkv_kept[:, i * kvw:(i + 1) * kvw], 0, 0).astype(BF)
-        stores.append(pltpu.make_async_copy(full, out, out_sem.at[QUAD + i]))
+        stores.append(pltpu.make_async_copy(full, out, out_sem.at[PIECES + i]))
         stores[-1].start()
     loads[3].wait()
-    stores.append(pltpu.make_async_copy(att_keep, att_out, out_sem.at[QUAD + 2]))
+    stores.append(pltpu.make_async_copy(att_keep, att_out, out_sem.at[PIECES + 2]))
     stores[-1].start()
     for cp in stores:
         cp.wait()
@@ -402,7 +404,7 @@
             pltpu.VMEM((rows, kvw), BF),
             pltpu.VMEM((keep, width), BF),
             dma((4,)),
-            dma((QUAD + 3,)),
+            dma((PIECES + 3,)),
         ],
         compiler_params=pltpu.CompilerParams(vmem_limit_bytes=64 * 1024 * 1024),
     )(att, dq_kept, dkv_kept, sel)

time: 23.4 us -> 23.5 us (level)
  no operation moved by 1% of the time
where the time goes in v5:
time: 23.5 us; the launch traced here: 23.2 us
  Pallas kernels  22.6 us (96%)
  between operations  0.64 us (3%)
    pallas_call x1, Pallas kernels, body(): pl.pallas_call(functools.partial(kernel, n, keep), out_shape=(jax.ShapeDt...  20 us
    pallas_call x1, Pallas kernels, body(): pl.pallas_call(spread_kernel, out_shape=(jax.ShapeDtypeStruct((keep, widt...  2.61 us

profile of v5, /device:TPU:0, one launch (start us, length us, event | category | flops | bytes accessed | tf_op | source)
XLA Modules:
  0.0 23.2 jit_solution(12337165300771080148)
XLA Ops:
  0.6 20.0 %shard_map.84 = (bf16[16,4096]{1,0:T(8,128)(2,1)}, bf16[16,4096]{1,0:T(8,128)(2,1)}, bf16[16,1024]{1,0:T(8,128)(2,1)}, bf16[16,192]{1,0:T(8,128)(2,1)}) custom-call(bf16[192,4096]{1,0:T(8,128)(2,1)} %q_hbm.1, bf16[192,512]{1,0:T(8,128)(2,1)} %k_hbm.1, bf16[192,512]{1,0:T(8,128)(2,1)} %v_hbm.1, s32[1,192]{1,0:T(1,128)} %rank_ref.1, bf16[16,4096]{1,0:T(8,128)(2,1)} %g_hbm.1), custom_call_target="tpu_custom_call" | custom-call | tf_op jit(solution)/shard_map/pallas_call | solution.py:342
  20.6 2.6 %shard_map.85 = (bf16[16,4096]{1,0:T(8,128)(2,1)}, bf16[192,4096]{1,0:T(8,128)(2,1)}, bf16[192,512]{1,0:T(8,128)(2,1)}, bf16[192,512]{1,0:T(8,128)(2,1)}) custom-call(bf16[16,4096]{1,0:T(8,128)(2,1)} %get-tuple-element.8.att_in, bf16[16,4096]{1,0:T(8,128)(2,1)} %get-tuple-element.9.dq_in, bf16[16,1024]{1,0:T(8,128)(2,1)} %get-tuple-element.10.dkv_in, ...), custom_call_target="tpu_custom_call" | custom-call | tf_op jit(solution)/shard_map/pallas_call | solution.py:388
